TPU v7x, 32 devices: a whole 2x2x4 slice. The times are simulated.
32 devices in a mesh: seq: 16 (over z, y, core), head: 2 (over x).
Axes of the slice: x: 2, y: 2, z: 4, core: 2. Of those that a mesh axis runs over, the one named last changes fastest.
Arguments:
- tokens: bfloat16 [8192, 1024], P('seq', 'head'), may hold values from -6 to 6
- w_qkv: bfloat16 [1, 1024, 3, 1024], P(None, None, None, 'head'), may hold values from -0.1875 to 0.1875
- w_out: bfloat16 [1, 1024, 1024], P(None, 'head'), may hold values from -0.1875 to 0.1875
- gain_in: bfloat16 [1, 1024], replicated, may hold values from 0.099609375 to 1.8984375
- gain_mid: bfloat16 [1, 1024], P(None, 'head'), may hold values from 0.099609375 to 1.8984375
Outputs:
- hidden: bfloat16 [8192, 1024], P('seq', 'head')
All inputs are finite; a program needn't handle non-finite values.
Results may differ from a plain program's by a relative error of at most 0.014.
Values may be sent and summed in bfloat16 or wider, within the bound.
A program may use at most 192 MiB of HBM per device.

v0:
```python
import math

import jax
import jax.numpy as jnp
import numpy as np
from jax import lax
from jax.sharding import PartitionSpec as P

D = 1024
DH = 64


EPSILON = 1e-06
SQRT_TWO = math.sqrt(2.0)


def carried_in(shard, axis, join, neutral):
    place = lax.axis_index(axis)
    gathered = jax.tree.map(
        lambda a, kind: lax.all_gather(a.astype(kind), axis), shard, (jnp.bfloat16, jnp.bfloat16)
    )
    state = jax.tree.map(lambda a, e: jnp.zeros_like(a) + jnp.asarray(e, a.dtype), shard, neutral)

    def one(turn, state):
        return join(
            state,
            jax.tree.map(
                lambda a, own: lax.dynamic_index_in_dim(a, turn, 0, False).astype(own.dtype),
                gathered,
                shard,
            ),
        )

    return lax.fori_loop(0, place, one, state)


def expand(columns):
    width = columns.shape[1]
    first_ids, second_ids = np.triu_indices(width)
    factors = np.where(first_ids == second_ids, 1.0, SQRT_TWO).astype(np.float32)
    first_cols = jnp.take(columns, jnp.asarray(first_ids.astype(np.int32)), axis=1)
    second_cols = jnp.take(columns, jnp.asarray(second_ids.astype(np.int32)), axis=1)
    return jnp.asarray(factors)[None, :, None] * first_cols * second_cols


def add_pair(earlier, latter):
    return (earlier[0] + latter[0], earlier[1] + latter[1])


def shards(tokens, w_qkv, w_out, gain_in, gain_mid):
    hidden = tokens
    row_count = tokens.shape[0]
    local_heads = w_qkv.shape[3] // DH
    row_ids = jnp.arange(row_count, dtype=jnp.int32)
    causal = row_ids[:, None] >= row_ids[None, :]
    whole = lax.all_gather(hidden, "head", axis=1, tiled=True)
    wide = whole.astype(jnp.float32)
    normed = (
        wide
        * lax.rsqrt(jnp.mean(wide * wide, axis=1, keepdims=True) + EPSILON)
        * gain_in[0].astype(jnp.float32)
    ).astype(jnp.bfloat16)
    weight_heads = w_qkv[0].reshape(D, 3, local_heads, DH)
    projected = jnp.einsum(
        "td,dche->chet", normed, weight_heads, preferred_element_type=jnp.float32
    ).astype(jnp.bfloat16)
    query_cols = projected[0]
    key_cols = projected[1]
    value_cols = projected[2]
    key_feats = expand(key_cols.astype(jnp.float32)).astype(jnp.bfloat16)
    block_state = jnp.einsum(
        "hft,het->hfe", key_feats, value_cols, preferred_element_type=jnp.float32
    )
    block_norm = jnp.sum(key_feats, axis=2, dtype=jnp.float32)
    empty = (jnp.zeros_like(block_state), jnp.zeros_like(block_norm))
    prefix_state, prefix_norm = carried_in((block_state, block_norm), "seq", add_pair, empty)
    query_feats = (expand(query_cols.astype(jnp.float32)) / DH).astype(jnp.bfloat16)
    scores = jnp.einsum("hdt,hds->hts", query_cols, key_cols, preferred_element_type=jnp.float32)
    weights = jnp.where(causal[None], scores * scores / DH, 0.0)
    local_den = jnp.sum(weights, axis=2)
    local_num = jnp.einsum(
        "hts,hes->the", weights.astype(jnp.bfloat16), value_cols, preferred_element_type=jnp.float32
    )
    num_prefix = jnp.einsum(
        "hft,hfe->the",
        query_feats,
        prefix_state.astype(jnp.bfloat16),
        preferred_element_type=jnp.float32,
    )
    den_prefix = jnp.einsum(
        "hft,hf->th",
        query_feats,
        prefix_norm.astype(jnp.bfloat16),
        preferred_element_type=jnp.float32,
    )
    attended = (local_num + num_prefix) / (1.0 + local_den.T + den_prefix)[:, :, None]
    attended = attended.reshape(row_count, local_heads * DH)
    row_block = lax.all_to_all(
        attended.astype(jnp.bfloat16), "head", split_axis=0, concat_axis=1, tiled=True
    ).astype(attended.dtype)
    inverse_rms = lax.rsqrt(jnp.mean(row_block * row_block, axis=1, keepdims=True) + EPSILON)
    weight_rows = lax.all_gather(w_out[0], "head", axis=0, tiled=True)
    gain_rows = lax.all_gather(gain_mid[0], "head", axis=0, tiled=True)
    mixed_in = (row_block * inverse_rms * gain_rows.astype(jnp.float32)).astype(jnp.bfloat16)
    summed = jnp.dot(mixed_in, weight_rows, preferred_element_type=jnp.float32)
    update = lax.all_to_all(
        summed.astype(jnp.bfloat16), "head", split_axis=1, concat_axis=0, tiled=True
    ).astype(summed.dtype)
    hidden = (hidden.astype(jnp.float32) + update).astype(jnp.bfloat16)
    return hidden


def solution(mesh):
    placed = (
        P("seq", "head"),
        P(None, None, None, "head"),
        P(None, "head", None),
        P(),
        P(None, "head"),
    )
    return jax.shard_map(
        shards, mesh=mesh, in_specs=placed, out_specs=P("seq", "head"), check_vma=False
    )
```

profile of v0, /device:TPU:29, one launch (start us, length us, event | category | flops | bytes accessed | tf_op | source)
XLA Modules:
  0.0 584.9 jit_solution(3213363271103893639)
XLA Ops:
  7.3 3.2 copy.55
  12.6 18.6 %all-gather.8.cloned.1.call-done = bf16[512,1024]{1,0:T(8,128)(2,1)} async-done(((bf16[512,512]{1,0:T(8,128)(2,1)}), bf16[512,1024]{1,0:T(8,128)(2,1)}) %all-gather.8.cloned.1.call-update) | async-done | bytes 1048592 | tf_op jit(solution)/shard_map/all_gather | solution.py:56
  32.7 3.2 fusion.48
  38.0 12.2 %gather_fusion = f32[2080,8,512]{2,1,0:T(8,128)} fusion(f32[8,64,512]{2,0,1:T(8,128)S(1)} %copy.57, s32[3072]{0:T(1024)S(1)} %pad_clamp_fusion.1), kind=kCustom, calls=%fused_computation.clone | custom fusion | bytes 68165760 | tf_op jit(solution)/shard_map/jit(_take)/gather | solution.py:41
  50.2 12.2 %gather_fusion.1 = f32[2080,8,512]{2,1,0:T(8,128)} fusion(f32[8,64,512]{2,0,1:T(8,128)S(1)} %copy.57, s32[3072]{0:T(1024)S(1)} %pad_clamp_fusion), kind=kCustom, calls=%fused_computation.1.clone | custom fusion | bytes 68165760 | tf_op jit(solution)/shard_map/jit(_take)/gather | solution.py:42
  62.3 29.1 %fusion.62 = (bf16[8,2080]{0,1:T(8,128)(2,1)S(1)}, bf16[8,2080,512]{2,0,1:T(8,128)(2,1)}) fusion(f32[2080,8,512]{2,1,0:T(8,128)} %gather_fusion.1, f32[2080,8,512]{2,1,0:T(8,128)} %gather_fusion, f32[2080]{0:T(1024)S(1)} %copy-done.2), kind=kLoop, calls=%fused_computation.69 | loop fusion | flops 34062080 | bytes 85238400 | tf_op jit(solution)/shard_map/reduce_sum | solution.py:74
  91.4 17.2 %fusion.11 = bf16[8,2080,64]{1,2,0:T(8,128)(2,1)} fusion(bf16[8,2080,512]{2,0,1:T(8,128)(2,1)} %get-tuple-element.85, bf16[3,8,64,512]{3,2,1,0:T(8,128)(2,1)S(1)} %convert_bitcast_fusion), kind=kOutput, calls=%fused_computation.23 | convolution fusion | flops 1091584000 | bytes 19693568 | tf_op jit(solution)/shard_map/hft,het->hfe/dot_general | solution.py:71
  109.4 1.8 copy.62
  111.3 13.4 %gather_fusion.2 = f32[2080,8,512]{2,1,0:T(8,128)} fusion(f32[8,64,512]{2,0,1:T(8,128)S(1)} %copy.62, s32[3072]{0:T(1024)S(1)} %pad_clamp_fusion.1), kind=kCustom, calls=%fused_computation.2.clone | custom fusion | bytes 68165760 | tf_op jit(solution)/shard_map/jit(_take)/gather | solution.py:41
  124.7 12.4 %gather_fusion.3 = f32[2080,8,512]{2,1,0:T(8,128)} fusion(f32[8,64,512]{2,0,1:T(8,128)S(1)} %copy.62, s32[3072]{0:T(1024)S(1)} %pad_clamp_fusion), kind=kCustom, calls=%fused_computation.3.clone | custom fusion | bytes 68165760 | tf_op jit(solution)/shard_map/jit(_take)/gather | solution.py:42
  137.3 21.7 %all-gather.1 = bf16[128,2080]{1,0:T(8,128)(2,1)} all-gather(bf16[8,2080]{1,0:T(8,128)(2,1)S(1)} %copy.60), channel_id=3, replica_groups=mesh['seq'=16,'head'=2] {'seq'}, dimensions={0}, use_global_device_ids=true | all-gather | bytes 565760 | tf_op jit(solution)/shard_map/all_gather | solution.py:20
  160.7 2.2 fusion.15
  162.9 29.3 %fusion.1 = bf16[8,2080,512]{2,0,1:T(8,128)(2,1)} fusion(f32[2080,8,512]{2,1,0:T(8,128)} %gather_fusion.3, f32[2080,8,512]{2,1,0:T(8,128)} %gather_fusion.2, f32[2080]{0:T(1024)S(1)} %copy-done.2), kind=kLoop, calls=%fused_computation.9 | loop fusion | flops 34078720 | bytes 85205120 | tf_op jit(solution)/shard_map/convert_element_type | solution.py:77
  192.3 98.8 %all-gather.10.cloned.1.call-done = bf16[128,2080,64]{1,2,0:T(8,128)(2,1)} async-done(((bf16[8,2080,64]{1,2,0:T(8,128)(2,1)}), bf16[128,2080,64]{1,2,0:T(8,128)(2,1)}) %all-gather.10.cloned.1.call-update) | async-done | bytes 34078736 | tf_op jit(solution)/shard_map/all_gather | solution.py:20
  291.1 4.1 broadcast_in_dim.39
  295.1 227.8 %while.12 = (s32[]{:T(128)}, f32[8,2080,64]{2,1,0:T(8,128)}, f32[8,2080]{1,0:T(8,128)S(1)}, s32[]{:T(128)}, bf16[16,8,2080,64]{2,3,1,0:T(8,128)(2,1)}, /*index=5...) while((s32[]{:T(128)}, f32[8,2080,64]{2,1,0:T(8,128)}, f32[8,2080]{1,0:T(8,128)S(1)}, ...), condition=%wide.region_3.5_spmd, body=%wide.region_2.4_spmd.sunk | while | flops 2163205 | bytes 19335816 | solution.py:34
  296.9 3.8 copy.96
  300.8 9.4 %convert_add_fusion.4 = f32[8,2080,64]{2,1,0:T(8,128)} fusion(f32[8,2080,64]{2,1,0:T(8,128)} %get-tuple-element.138, bf16[1,8,2080,64]{3,2,1,0:T(8,128)(2,1)} %copy.96), kind=kLoop, calls=%fused_computation.4.clone.1 | loop fusion | flops 2129920 | bytes 10649600 | tf_op jit(solution)/shard_map/while/body/add | solution.py:47
  310.9 1.8 constant_dynamic-slice_fusion.2
  312.7 3.8 copy.96
  316.6 8.7 %convert_add_fusion.4 = f32[8,2080,64]{2,1,0:T(8,128)} fusion(f32[8,2080,64]{2,1,0:T(8,128)} %get-tuple-element.138, bf16[1,8,2080,64]{3,2,1,0:T(8,128)(2,1)} %copy.96), kind=kLoop, calls=%fused_computation.4.clone.1 | loop fusion | flops 2129920 | bytes 10649600 | tf_op jit(solution)/shard_map/while/body/add | solution.py:47
  326.1 1.8 constant_dynamic-slice_fusion.2
  327.9 3.8 copy.96
  331.7 8.7 %convert_add_fusion.4 = f32[8,2080,64]{2,1,0:T(8,128)} fusion(f32[8,2080,64]{2,1,0:T(8,128)} %get-tuple-element.138, bf16[1,8,2080,64]{3,2,1,0:T(8,128)(2,1)} %copy.96), kind=kLoop, calls=%fused_computation.4.clone.1 | loop fusion | flops 2129920 | bytes 10649600 | tf_op jit(solution)/shard_map/while/body/add | solution.py:47
  341.2 1.8 constant_dynamic-slice_fusion.2
  343.0 3.8 copy.96
  346.8 8.7 %convert_add_fusion.4 = f32[8,2080,64]{2,1,0:T(8,128)} fusion(f32[8,2080,64]{2,1,0:T(8,128)} %get-tuple-element.138, bf16[1,8,2080,64]{3,2,1,0:T(8,128)(2,1)} %copy.96), kind=kLoop, calls=%fused_computation.4.clone.1 | loop fusion | flops 2129920 | bytes 10649600 | tf_op jit(solution)/shard_map/while/body/add | solution.py:47
  356.3 1.8 constant_dynamic-slice_fusion.2
  358.1 3.8 copy.96
  361.9 8.7 %convert_add_fusion.4 = f32[8,2080,64]{2,1,0:T(8,128)} fusion(f32[8,2080,64]{2,1,0:T(8,128)} %get-tuple-element.138, bf16[1,8,2080,64]{3,2,1,0:T(8,128)(2,1)} %copy.96), kind=kLoop, calls=%fused_computation.4.clone.1 | loop fusion | flops 2129920 | bytes 10649600 | tf_op jit(solution)/shard_map/while/body/add | solution.py:47
  371.5 1.8 constant_dynamic-slice_fusion.2
  373.2 3.8 copy.96
  377.1 8.7 %convert_add_fusion.4 = f32[8,2080,64]{2,1,0:T(8,128)} fusion(f32[8,2080,64]{2,1,0:T(8,128)} %get-tuple-element.138, bf16[1,8,2080,64]{3,2,1,0:T(8,128)(2,1)} %copy.96), kind=kLoop, calls=%fused_computation.4.clone.1 | loop fusion | flops 2129920 | bytes 10649600 | tf_op jit(solution)/shard_map/while/body/add | solution.py:47
  386.6 1.8 constant_dynamic-slice_fusion.2
  388.4 3.8 copy.96
  392.2 8.7 %convert_add_fusion.4 = f32[8,2080,64]{2,1,0:T(8,128)} fusion(f32[8,2080,64]{2,1,0:T(8,128)} %get-tuple-element.138, bf16[1,8,2080,64]{3,2,1,0:T(8,128)(2,1)} %copy.96), kind=kLoop, calls=%fused_computation.4.clone.1 | loop fusion | flops 2129920 | bytes 10649600 | tf_op jit(solution)/shard_map/while/body/add | solution.py:47
  401.7 1.8 constant_dynamic-slice_fusion.2
  403.5 3.8 copy.96
  407.3 8.7 %convert_add_fusion.4 = f32[8,2080,64]{2,1,0:T(8,128)} fusion(f32[8,2080,64]{2,1,0:T(8,128)} %get-tuple-element.138, bf16[1,8,2080,64]{3,2,1,0:T(8,128)(2,1)} %copy.96), kind=kLoop, calls=%fused_computation.4.clone.1 | loop fusion | flops 2129920 | bytes 10649600 | tf_op jit(solution)/shard_map/while/body/add | solution.py:47
  416.8 1.8 constant_dynamic-slice_fusion.2
  418.6 3.8 copy.96
  422.5 8.7 %convert_add_fusion.4 = f32[8,2080,64]{2,1,0:T(8,128)} fusion(f32[8,2080,64]{2,1,0:T(8,128)} %get-tuple-element.138, bf16[1,8,2080,64]{3,2,1,0:T(8,128)(2,1)} %copy.96), kind=kLoop, calls=%fused_computation.4.clone.1 | loop fusion | flops 2129920 | bytes 10649600 | tf_op jit(solution)/shard_map/while/body/add | solution.py:47
  432.0 1.8 constant_dynamic-slice_fusion.2
  433.8 3.8 copy.96
  437.6 8.7 %convert_add_fusion.4 = f32[8,2080,64]{2,1,0:T(8,128)} fusion(f32[8,2080,64]{2,1,0:T(8,128)} %get-tuple-element.138, bf16[1,8,2080,64]{3,2,1,0:T(8,128)(2,1)} %copy.96), kind=kLoop, calls=%fused_computation.4.clone.1 | loop fusion | flops 2129920 | bytes 10649600 | tf_op jit(solution)/shard_map/while/body/add | solution.py:47
  447.1 1.8 constant_dynamic-slice_fusion.2
  448.9 3.8 copy.96
  452.7 8.7 %convert_add_fusion.4 = f32[8,2080,64]{2,1,0:T(8,128)} fusion(f32[8,2080,64]{2,1,0:T(8,128)} %get-tuple-element.138, bf16[1,8,2080,64]{3,2,1,0:T(8,128)(2,1)} %copy.96), kind=kLoop, calls=%fused_computation.4.clone.1 | loop fusion | flops 2129920 | bytes 10649600 | tf_op jit(solution)/shard_map/while/body/add | solution.py:47
  462.2 1.8 constant_dynamic-slice_fusion.2
  464.0 3.8 copy.96
  467.9 8.7 %convert_add_fusion.4 = f32[8,2080,64]{2,1,0:T(8,128)} fusion(f32[8,2080,64]{2,1,0:T(8,128)} %get-tuple-element.138, bf16[1,8,2080,64]{3,2,1,0:T(8,128)(2,1)} %copy.96), kind=kLoop, calls=%fused_computation.4.clone.1 | loop fusion | flops 2129920 | bytes 10649600 | tf_op jit(solution)/shard_map/while/body/add | solution.py:47
  477.4 1.8 constant_dynamic-slice_fusion.2
  479.2 3.8 copy.96
  483.0 8.7 %convert_add_fusion.4 = f32[8,2080,64]{2,1,0:T(8,128)} fusion(f32[8,2080,64]{2,1,0:T(8,128)} %get-tuple-element.138, bf16[1,8,2080,64]{3,2,1,0:T(8,128)(2,1)} %copy.96), kind=kLoop, calls=%fused_computation.4.clone.1 | loop fusion | flops 2129920 | bytes 10649600 | tf_op jit(solution)/shard_map/while/body/add | solution.py:47
  494.3 3.8 copy.96
  498.1 8.7 %convert_add_fusion.4 = f32[8,2080,64]{2,1,0:T(8,128)} fusion(f32[8,2080,64]{2,1,0:T(8,128)} %get-tuple-element.138, bf16[1,8,2080,64]{3,2,1,0:T(8,128)(2,1)} %copy.96), kind=kLoop, calls=%fused_computation.4.clone.1 | loop fusion | flops 2129920 | bytes 10649600 | tf_op jit(solution)/shard_map/while/body/add | solution.py:47
  509.4 3.8 copy.96
  513.3 8.7 %convert_add_fusion.4 = f32[8,2080,64]{2,1,0:T(8,128)} fusion(f32[8,2080,64]{2,1,0:T(8,128)} %get-tuple-element.138, bf16[1,8,2080,64]{3,2,1,0:T(8,128)(2,1)} %copy.96), kind=kLoop, calls=%fused_computation.4.clone.1 | loop fusion | flops 2129920 | bytes 10649600 | tf_op jit(solution)/shard_map/while/body/add | solution.py:47
  523.0 14.9 %fusion.5 = f32[8,1,512]{2,1,0:T(1,128)S(1)} fusion(bf16[8,2080,512]{2,0,1:T(8,128)(2,1)} %fusion.1, bf16[8,2080,1]{1,0,2:T(8,128)(2,1)S(1)} %convert_bitcast_fusion.1), kind=kOutput, calls=%fused_computation.16 | convolution fusion | flops 17039360 | bytes 17089024 | tf_op jit(solution)/shard_map/hft,hf->th/dot_general | solution.py:90
  537.9 18.2 %fusion.43 = bf16[512,8,64]{0,2,1:T(8,128)(2,1)S(1)} fusion(f32[8,64,512]{2,1,0:T(8,128)S(1)} %copy-done, bf16[8,2080,512]{2,0,1:T(8,128)(2,1)} %fusion.1, f32[8,2080,64]{2,1,0:T(8,128)} %get-tuple-element.40, f32[512,8]{0,1:T(8,128)S(1)} %fusion.59), kind=kOutput, calls=%fused_computation.41 | convolution fusion | flops 1092370432 | bytes 22888448 | tf_op jit(solution)/shard_map/hft,hfe->the/dot_general | solution.py:84
  557.1 3.5 all-to-all-start
  560.6 5.8 all-gather.2
  566.8 2.3 fusion.40
  569.2 7.8 %all_to_all.23 = bf16[256,2,512]{2,0,1:T(8,128)(2,1)S(1)} all-to-all(bf16[256,2,512]{2,0,1:T(8,128)(2,1)S(1)} %bitcast.102), channel_id=1, replica_groups=mesh['seq'=16,'head'=2] {'head'}, dimensions={1} | all-to-all | bytes 1048576 | tf_op jit(solution)/shard_map/all_to_all | solution.py:106
  (56 shorter events, 28.6 us)
Async XLA Ops:
  6.5 24.6 %all-gather.8.cloned.1.call-start = ((), (), s32[]{:S(2)}) async-start(), calls=%async_computation.2 | async-start | bytes 1572864 | tf_op jit(solution)/shard_map/all_gather | solution.py:56
  7.3 283.8 %all-gather.10.cloned.1.call-start = ((), (), s32[]{:S(2)}) async-start(), calls=%async_computation.3 | async-start | bytes 37879808 | tf_op jit(solution)/shard_map/all_gather | solution.py:20
  50.2 12.2 %copy-start.2 = (f32[2080]{0:T(1024)S(1)}, f32[2080]{0:T(1024)}, u32[]{:S(2)}) copy-start(f32[2080]{0:T(1024)} %constant.59.clone) | copy-start | bytes 24964
  108.6 458.2 %all-gather.12.cloned.1.call-start = ((), (), s32[]{:S(2)}) async-start(), calls=%async_computation.4 | async-start | bytes 3145728 | tf_op jit(solution)/shard_map/all_gather | solution.py:102
  523.0 14.9 %copy-start = (f32[8,64,512]{2,1,0:T(8,128)S(1)}, f32[8,64,512]{2,1,0:T(8,128)}, u32[]{:S(2)}) copy-start(f32[8,64,512]{2,1,0:T(8,128)} %fusion.15) | copy-start | bytes 3145732
  537.9 22.7 %copy-start.3 = (bf16[1,512]{1,0:T(2,128)(2,1)S(1)}, bf16[1,512]{1,0:T(2,128)(2,1)}, u32[]{:S(2)}) copy-start(bf16[1,512]{1,0:T(2,128)(2,1)} %param.19) | copy-start | bytes 3076
  556.0 21.0 %copy-start.1 = (bf16[512,512]{1,0:T(8,128)(2,1)S(1)}, bf16[512,512]{1,0:T(8,128)(2,1)}, u32[]{:S(2)}) copy-start(bf16[512,512]{1,0:T(8,128)(2,1)} %param.15) | copy-start | bytes 1572868
  557.1 9.3 %all-to-all-start = ((bf16[2,256,512]{1,2,0:T(8,128)(2,1)}), bf16[2,256,512]{1,2,0:T(8,128)(2,1)S(1)}, u32[]{:S(2)}, u32[]{:S(2)}) async-start(bf16[2,256,512]{1,2,0:T(8,128)(2,1)} %copy.66), calls=%async_computation | async-start | bytes 1048576 | tf_op jit(solution)/shard_map/all_to_all | solution.py:98
Sparse Core Ops, SparseCore 0:
  8.9 22.2 all-gather.7
  108.7 182.3 all-gather.9
  292.6 33.9 all-gather.11
where the time goes:
time: 592 us; the launch traced here: 585 us
  other arithmetic  208 us (35%)
  local copies, waits for them, and re-layouts  145 us (24%)
  waiting for transfers between devices  119 us (20%)
  matrix products  59.7 us (10%)
  blocking collectives  35.3 us (6%)
  between operations  13.7 us (2%)
    add x30, other arithmetic, add_pair(): return (earlier[0] + latter[0], earlier[1] + latter[1])  143 us
    all_gather x1, waiting for transfers between devices, carried_in(): lax.all_gather(a.astype(kind), axis)  98.8 us
    dynamic_slice x30, local copies, waits for them, and re-layouts, one(): lax.dynamic_index_in_dim(a, turn, 0, False).astype(own.dtype)  84.3 us
    convert_element_type x1, other arithmetic, shards(): (expand(query_cols.astype(jnp.float32)) / DH).astype(jnp.bfloat16)  29.3 us
    reduce_sum x1, other arithmetic, shards(): block_norm = jnp.sum(key_feats, axis=2, dtype=jnp.float32)  29.1 us
    gather x2, local copies, waits for them, and re-layouts, expand(): jnp.take(columns, jnp.asarray(first_ids.astype(np.int32)), axis=1)  25.6 us
    gather x2, local copies, waits for them, and re-layouts, expand(): jnp.take(columns, jnp.asarray(second_ids.astype(np.int32)), axis=1)  24.5 us
    all_gather x1, blocking collectives, carried_in(): lax.all_gather(a.astype(kind), axis)  21.7 us
  transfers between devices with their start and end apart: 4, of which 2 were waited for; matrix products, arithmetic and copies ran while one was open for 57% of the time, Pallas kernels for 0%

commit v1 on v0

v1 whole, which is shorter than its diff:
```python
import functools

import jax
import jax.numpy as jnp
from jax import lax
from jax.experimental import pallas as pl
from jax.experimental.pallas import tpu as pltpu
from jax.sharding import PartitionSpec as P

DH = 64
EPSILON = 1e-06
MESH = pl.DeviceIdType.MESH
OFFSETS = DH // 2 + 1
FEATS = OFFSETS * DH
ROWS = FEATS + DH
PARTS = 4


def dot(a, b, dims=((1,), (0,))):
    return lax.dot_general(a, b, (dims, ((), ())), preferred_element_type=jnp.float32)


def kernel(
    n, nx, x_ref, w_ref, wo_ref, gain_in_ref, gain_mid_ref, out_ref,
    xbuf, q_t, k_t, v_t, v_pair, feat, twice, state, prefix, outgoing, num, den, att, ss, part_out, part_in,
    x_send, x_recv, chain_send, chain_recv, ss_send, ss_recv, part_send, part_recv,
):
    me = lax.axis_index("seq")
    hx = lax.axis_index("head")
    rows, width = x_ref.shape
    features = w_ref.shape[2]
    heads = features // DH
    pairs = heads // 2
    full = nx * width
    piece = ROWS // PARTS
    right, left = lax.rem(me + 1, n), lax.rem(me + n - 1, n)

    barrier = pltpu.get_barrier_semaphore()
    for neighbour in (left, right):
        pl.semaphore_signal(barrier, inc=1, device_id=(neighbour, hx), device_id_type=MESH)
    for k in range(1, nx):
        pl.semaphore_signal(
            barrier, inc=1, device_id=(me, lax.rem(hx + k, nx)), device_id_type=MESH
        )
    pl.semaphore_wait(barrier, 2 + nx - 1)

    def token_copy(k):
        return pltpu.make_async_remote_copy(
            src_ref=x_ref, dst_ref=xbuf.at[hx], send_sem=x_send.at[k], recv_sem=x_recv.at[k],
            device_id=(me, lax.rem(hx + k, nx)), device_id_type=MESH,
        )

    for k in range(1, nx):
        token_copy(k).start()
    xbuf[hx] = x_ref[...]
    for k in range(1, nx):
        token_copy(k).wait()

    total = jnp.zeros((rows, 1), jnp.float32)
    for j in range(nx):
        wide = xbuf[j].astype(jnp.float32)
        total = total + jnp.sum(wide * wide, axis=1, keepdims=True)
    inverse = lax.rsqrt(total / full + EPSILON)
    for j in range(nx):
        gain = gain_in_ref[:, j * width:(j + 1) * width].astype(jnp.float32)
        xbuf[j] = (xbuf[j].astype(jnp.float32) * inverse * gain).astype(jnp.bfloat16)
    for c in range(3):
        y = dot(xbuf[0], w_ref[c, :width, :])
        for j in range(1, nx):
            y = y + dot(xbuf[j], w_ref[c, j * width:(j + 1) * width, :])
        y = y.astype(jnp.bfloat16)
        flipped = y.T.reshape(heads, DH, rows)
        (q_t, k_t, v_t)[c][...] = flipped
        if c == 2:
            for p in range(pairs):
                v_pair[p] = y[:, p * 2 * DH:(p + 1) * 2 * DH]

    low_lane = lax.broadcasted_iota(jnp.int32, (1, 2 * DH), 1) < DH

    def expand(u, edge, middle):
        wide = u.astype(jnp.float32)
        twice[:DH, :] = wide
        twice[DH:, :] = wide
        for d in range(OFFSETS):
            scaled = edge if d in (0, OFFSETS - 1) else middle
            feat[d * DH:(d + 1) * DH, :] = scaled * twice[d:d + DH, :].astype(jnp.bfloat16)

    def make_state(p):
        both = jnp.concatenate([k_t[2 * p], k_t[2 * p + 1]], axis=0)
        values = v_pair[p]
        for a in range(2):
            u = k_t[2 * p + a]
            expand(u, u, u)
            step = FEATS // PARTS
            for i in range(PARTS):
                at = slice(i * step, (i + 1) * step)
                got = dot(feat[at, :], values)
                state[p, at, :] = got if a == 0 else jnp.where(low_lane, state[p, at, :], got)
            gram = dot(u, both, ((1,), (1,)))
            at = slice(FEATS, ROWS)
            state[p, at, :] = gram if a == 0 else jnp.where(low_lane, state[p, at, :], gram)

    causal = lax.broadcasted_iota(jnp.int32, (rows, rows), 0) <= lax.broadcasted_iota(
        jnp.int32, (rows, rows), 1
    )

    def local(h, carry):
        scores = dot(k_t[h], q_t[h], ((0,), (0,)))
        weights = jnp.where(causal, scores * scores * (1.0 / DH), 0.0)
        den[h] = jnp.sum(weights, axis=0, keepdims=True)
        num[h] = dot(v_t[h], weights.astype(jnp.bfloat16))
        return carry

    def chain_copy(p, i):
        return pltpu.make_async_remote_copy(
            src_ref=outgoing.at[p, i], dst_ref=prefix.at[p, i],
            send_sem=chain_send.at[p, i], recv_sem=chain_recv.at[p, i],
            device_id=(right, hx), device_id_type=MESH,
        )

    @pl.when(me == 0)
    def _():
        prefix[...] = jnp.zeros_like(prefix)

    make_state(0)
    late = me >= n // 2
    lax.fori_loop(0, jnp.where(late, heads, 0), local, 0)

    def turn(p, carry):
        @pl.when(p + 1 < pairs)
        def _():
            make_state(p + 1)

        for i in range(PARTS):
            copy = chain_copy(p, i)

            @pl.when(me > 0)
            def _():
                copy.wait_recv()

            @pl.when(me < n - 1)
            def _():
                own = state[p, i * piece:(i + 1) * piece, :]
                outgoing[p, i] = (prefix[p, i].astype(jnp.float32) + own).astype(jnp.bfloat16)
                copy.start()

        whole = prefix[p].reshape(ROWS, 2 * DH).T
        for a in range(2):
            h = 2 * p + a
            u = q_t[h]
            expand(u, u * (1.0 / DH), u * (2.0 / DH))
            mine = whole[a * DH:(a + 1) * DH, :]
            num[h] = num[h] + dot(mine[:, :FEATS], feat[...])
            gram = dot(mine[:, FEATS:], u)
            den[h] = den[h] + jnp.sum(
                gram * u.astype(jnp.float32), axis=0, keepdims=True
            ) * (1.0 / DH)
        return carry

    @pl.when(jnp.logical_not(late))
    def _():
        num[...] = jnp.zeros_like(num)
        den[...] = jnp.zeros_like(den)

    lax.fori_loop(0, pairs, turn, 0)

    def late_local(h, carry):
        old_num, old_den = num[h], den[h]
        local(h, carry)
        num[h] = num[h] + old_num
        den[h] = den[h] + old_den
        return carry

    lax.fori_loop(0, jnp.where(late, 0, heads), late_local, 0)

    attended = (num[...] / (1.0 + den[...])).reshape(features, rows)
    ss[0] = jnp.broadcast_to(jnp.sum(attended * attended, axis=0, keepdims=True), (8, rows))

    def ss_copy(k):
        return pltpu.make_async_remote_copy(
            src_ref=ss.at[0], dst_ref=ss.at[k], send_sem=ss_send.at[k], recv_sem=ss_recv.at[k],
            device_id=(me, lax.rem(hx + k, nx)), device_id_type=MESH,
        )

    def part_copy(k):
        return pltpu.make_async_remote_copy(
            src_ref=part_out.at[k], dst_ref=part_in.at[k], send_sem=part_send.at[k],
            recv_sem=part_recv.at[k],
            device_id=(me, lax.rem(hx + k, nx)), device_id_type=MESH,
        )

    for k in range(1, nx):
        ss_copy(k).start()
    att[...] = (attended.T * gain_mid_ref[...].astype(jnp.float32)).astype(jnp.bfloat16)
    for k in range(1, nx):
        at = pl.multiple_of(lax.rem(hx + k, nx) * width, width)
        part_out[k] = dot(att[...], wo_ref[:, pl.ds(at, width)]).astype(jnp.bfloat16)
        part_copy(k).start()
    update = dot(att[...], wo_ref[:, pl.ds(pl.multiple_of(hx * width, width), width)])
    for k in range(1, nx):
        ss_copy(k).wait()
    squares = ss[0]
    for k in range(1, nx):
        squares = squares + ss[k]
    columns = jnp.broadcast_to(squares[:1], (128, rows)).T[:, :1]
    scale = lax.rsqrt(columns / full + EPSILON)
    for k in range(1, nx):
        part_copy(k).wait()
        update = update + part_in[k].astype(jnp.float32)
    out_ref[...] = (x_ref[...].astype(jnp.float32) + update * scale).astype(jnp.bfloat16)

    @pl.when(me < n - 1)
    def _():
        for p in range(pairs):
            for i in range(PARTS):
                chain_copy(p, i).wait_send()


def shards(n, nx, tokens, w_qkv, w_out, gain_in, gain_mid):
    rows, width = tokens.shape
    features = w_qkv.shape[3]
    heads = features // DH
    pairs = heads // 2
    bf16, f32 = jnp.bfloat16, jnp.float32
    dma = pltpu.SemaphoreType.DMA
    return pl.pallas_call(
        functools.partial(kernel, n, nx),
        out_shape=jax.ShapeDtypeStruct((rows, width), bf16),
        in_specs=[pl.BlockSpec(memory_space=pltpu.VMEM)] * 5,
        out_specs=pl.BlockSpec(memory_space=pltpu.VMEM),
        scratch_shapes=[
            pltpu.VMEM((nx, rows, width), bf16),
            pltpu.VMEM((heads, DH, rows), bf16),
            pltpu.VMEM((heads, DH, rows), bf16),
            pltpu.VMEM((heads, DH, rows), bf16),
            pltpu.VMEM((pairs, rows, 2 * DH), bf16),
            pltpu.VMEM((FEATS, rows), bf16),
            pltpu.VMEM((2 * DH, rows), f32),
            pltpu.VMEM((pairs, ROWS, 2 * DH), f32),
            pltpu.VMEM((pairs, PARTS, ROWS // PARTS, 2 * DH), bf16),
            pltpu.VMEM((pairs, PARTS, ROWS // PARTS, 2 * DH), bf16),
            pltpu.VMEM((heads, DH, rows), f32),
            pltpu.VMEM((heads, 1, rows), f32),
            pltpu.VMEM((rows, features), bf16),
            pltpu.VMEM((nx, 8, rows), f32),
            pltpu.VMEM((nx, rows, width), bf16),
            pltpu.VMEM((nx, rows, width), bf16),
            dma((nx,)), dma((nx,)),
            dma((pairs, PARTS)), dma((pairs, PARTS)),
            dma((nx,)), dma((nx,)),
            dma((nx,)), dma((nx,)),
        ],
        compiler_params=pltpu.CompilerParams(
            collective_id=0, has_side_effects=True, vmem_limit_bytes=48 * 1024 * 1024
        ),
    )(tokens, w_qkv[0].transpose(1, 0, 2), w_out[0], gain_in, gain_mid)


def solution(mesh):
    placed = (
        P("seq", "head"),
        P(None, None, None, "head"),
        P(None, "head", None),
        P(),
        P(None, "head"),
    )
    return jax.shard_map(
        functools.partial(shards, mesh.shape["seq"], mesh.shape["head"]),
        mesh=mesh, in_specs=placed, out_specs=P("seq", "head"), check_vma=False,
    )
```

time: 592 us -> 104 us (0.18); the launches traced: 585 us -> 104 us
  other arithmetic: 208 us -> 0 us
  local copies, waits for them, and re-layouts: 145 us -> 6.32 us
  waiting for transfers between devices: 119 us -> 0 us
  Pallas kernels: 0 us -> 97.2 us
  matrix products: 59.7 us -> 0 us
  blocking collectives: 35.3 us -> 0 us
  between operations: 13.7 us -> 0.01 us
    add x31 -> x0, other arithmetic: 143 us -> none  [the longest x30 143 us: add_pair(): return (earlier[0] + latter[0], earlier[1] + latter[1])]
    all_gather x3 -> x0, waiting for transfers between devices: 117 us -> none  [the longest x1 98.8 us: carried_in(): lax.all_gather(a.astype(kind), axis)]
    pallas_call x0 -> x1, Pallas kernels: none -> 97.2 us  [shards(): pl.pallas_call(functools.partial(kernel, n, nx), out_shape=jax.ShapeDtype...]
    dynamic_slice x30 -> x0, local copies, waits for them, and re-layouts: 84.3 us -> none  [one(): lax.dynamic_index_in_dim(a, turn, 0, False).astype(own.dtype)]
    dot_general x6 -> x0, matrix products: 56.5 us -> none  [the longest x1 18.2 us: shards(): jnp.einsum('hft,hfe->the', query_feats, prefix_state.astype(jnp.bfloat16)...]
    gather x4 -> x0, local copies, waits for them, and re-layouts: 50.2 us -> none  [the longest x2 25.6 us: expand(): jnp.take(columns, jnp.asarray(first_ids.astype(np.int32)), axis=1)]
    convert_element_type x7 -> x0, other arithmetic: 32 us -> none  [the longest x1 29.3 us: shards(): (expand(query_cols.astype(jnp.float32)) / DH).astype(jnp.bfloat16)]
    reduce_sum x3 -> x0, other arithmetic: 30.7 us -> none  [the longest x1 29.1 us: shards(): block_norm = jnp.sum(key_feats, axis=2, dtype=jnp.float32)]
  transfers between devices with their start and end apart: 4 -> 0, of which waited for: 2 -> 0; matrix products, arithmetic and copies ran while one was open for 57% -> 0% of each run, Pallas kernels for 0% -> 0%
where the time goes in v1:
time: 104 us
  Pallas kernels  97.2 us (93%)
  local copies, waits for them, and re-layouts  6.32 us (6%)
    pallas_call x1, Pallas kernels, shards(): pl.pallas_call(functools.partial(kernel, n, nx), out_shape=jax.ShapeDtype...  97.2 us
    unnamed x11, local copies, waits for them, and re-layouts  6.32 us

profile of v1, /device:TPU:29, one launch (start us, length us, event | category | flops | bytes accessed | tf_op | source)
XLA Modules:
  0.0 103.6 jit_solution(14078574936942616691)
XLA Ops:
  0.0 0.0 copy-start
  0.0 1.9 %copy-done = bf16[1,1024,3,512]{3,1,2,0:T(8,128)(2,1)S(1)} copy-done((bf16[1,1024,3,512]{3,1,2,0:T(8,128)(2,1)S(1)}, bf16[1,1024,3,512]{3,1,2,0:T(8,128)(2,1)}, u32[]{:S(2)}) %copy-start) | copy-done | bytes 3145752
  1.9 0.0 copy-start.1
  1.9 1.2 %copy-done.1 = bf16[1,512,1024]{2,1,0:T(8,128)(2,1)S(1)} copy-done((bf16[1,512,1024]{2,1,0:T(8,128)(2,1)S(1)}, bf16[1,512,1024]{2,1,0:T(8,128)(2,1)}, u32[]{:S(2)}) %copy-start.1) | copy-done | bytes 1048600
  3.1 0.0 copy-start.2
  3.1 1.0 %copy-done.2 = bf16[512,512]{1,0:T(8,128)(2,1)S(1)} copy-done((bf16[512,512]{1,0:T(8,128)(2,1)S(1)}, bf16[512,512]{1,0:T(8,128)(2,1)}, u32[]{:S(2)}) %copy-start.2) | copy-done | bytes 524312
  4.2 0.0 copy-start.3
  4.2 0.7 copy-done.3
  4.8 0.0 copy-start.4
  4.8 0.7 copy-done.4
  5.5 97.2 %shard_map.55 = bf16[512,512]{1,0:T(8,128)(2,1)S(1)} custom-call(bf16[512,512]{1,0:T(8,128)(2,1)S(1)} %copy-done.2, bf16[3,1024,512]{2,1,0:T(8,128)(2,1)S(1)} %bitcast.4, bf16[512,1024]{1,0:T(8,128)(2,1)S(1)} %bitcast.5, bf16[1,1024]{1,0:T(2,128)(2,1)S(1)} %copy-done.3, bf16[1,512]{1,0:T(2,128)(2,1)S(1)} %copy-done.4), custom_call_target="tpu_custom_call" | custom-call | tf_op jit(solution)/shard_map/pallas_call | solution.py:226
  102.8 0.8 copy.7
Async XLA Ops:
  0.0 1.9 %copy-start = (bf16[1,1024,3,512]{3,1,2,0:T(8,128)(2,1)S(1)}, bf16[1,1024,3,512]{3,1,2,0:T(8,128)(2,1)}, u32[]{:S(2)}) copy-start(bf16[1,1024,3,512]{3,1,2,0:T(8,128)(2,1)} %param.6) | copy-start | bytes 9437188
  1.9 1.2 %copy-start.1 = (bf16[1,512,1024]{2,1,0:T(8,128)(2,1)S(1)}, bf16[1,512,1024]{2,1,0:T(8,128)(2,1)}, u32[]{:S(2)}) copy-start(bf16[1,512,1024]{2,1,0:T(8,128)(2,1)} %param.7) | copy-start | bytes 3145732
  3.1 1.0 %copy-start.2 = (bf16[512,512]{1,0:T(8,128)(2,1)S(1)}, bf16[512,512]{1,0:T(8,128)(2,1)}, u32[]{:S(2)}) copy-start(bf16[512,512]{1,0:T(8,128)(2,1)} %x_ref.1) | copy-start | bytes 1572868
  4.2 0.7 copy-start.3
  4.8 0.7 copy-start.4

commit v2 on v1

v2 whole, which is shorter than its diff:
```python
import functools

import jax
import jax.numpy as jnp
from jax import lax
from jax.experimental import pallas as pl
from jax.experimental.pallas import tpu as pltpu
from jax.sharding import PartitionSpec as P

DH = 64
EPSILON = 1e-06
MESH = pl.DeviceIdType.MESH
TILE = 16
FEATS = DH * (DH // 2 + 1)
ROWS = FEATS + DH
PARTS = 8


def dot(a, b, dims=((1,), (0,))):
    return lax.dot_general(a, b, (dims, ((), ())), preferred_element_type=jnp.float32)


def feature_tiles():
    tiles = []
    for r in range(TILE):
        for b in range(DH // TILE):
            for a in range(b + 1):
                if a < b or r <= TILE // 2:
                    tiles.append((a, b, r))
    return tiles


def kernel(
    n, nx, x_ref, w_hbm, wo_hbm, gain_in_ref, gain_mid_ref, out_ref,
    x_own, w_ref, wo_ref, wo_in, xbuf, q_t, k_t, v_t, v_pair, feat, twice, state, prefix, outgoing,
    num, den, att, att_in, ss,
    load_sem, x_send, x_recv, wo_send, wo_recv, chain_send, chain_recv, ss_send, ss_recv,
    att_send, att_recv,
):
    me = lax.axis_index("seq")
    hx = lax.axis_index("head")
    rows, width = x_own.shape
    features = w_ref.shape[2]
    heads = features // DH
    pairs = heads // 2
    full = nx * width
    piece = ROWS // PARTS
    right, left = lax.rem(me + 1, n), lax.rem(me + n - 1, n)

    def load(src, dst, i):
        return pltpu.make_async_copy(src, dst, load_sem.at[i])

    load(x_ref, x_own, 0).start()
    load(w_hbm, w_ref, 1).start()
    load(wo_hbm, wo_ref, 2).start()

    barrier = pltpu.get_barrier_semaphore()
    for neighbour in (left, right):
        pl.semaphore_signal(barrier, inc=1, device_id=(neighbour, hx), device_id_type=MESH)
    for k in range(1, nx):
        pl.semaphore_signal(
            barrier, inc=1, device_id=(me, lax.rem(hx + k, nx)), device_id_type=MESH
        )
    pl.semaphore_wait(barrier, 2 + nx - 1)

    def across(src, dst, send, recv, k):
        return pltpu.make_async_remote_copy(
            src_ref=src, dst_ref=dst, send_sem=send, recv_sem=recv,
            device_id=(me, lax.rem(hx + k, nx)), device_id_type=MESH,
        )

    def token_copy(k):
        return across(x_ref, xbuf.at[hx], x_send.at[k], x_recv.at[k], k)

    def wo_copy(k):
        at = pl.multiple_of(lax.rem(hx + k, nx) * width, width)
        return across(
            wo_ref.at[:, pl.ds(at, width)], wo_in.at[k], wo_send.at[k], wo_recv.at[k], k
        )

    def ss_copy(k):
        return across(ss.at[0], ss.at[k], ss_send.at[k], ss_recv.at[k], k)

    def att_copy(k, p):
        return across(att.at[p], att_in.at[k, p], att_send.at[k, p], att_recv.at[k, p], k)

    for k in range(1, nx):
        token_copy(k).start()

    num[...] = jnp.zeros_like(num)
    den[...] = jnp.zeros_like(den)
    ss[0] = jnp.zeros_like(ss[0])

    @pl.when(me == 0)
    def _():
        prefix[...] = jnp.zeros_like(prefix)

    load(x_ref, x_own, 0).wait()
    xbuf[hx] = x_own[...]
    load(w_hbm, w_ref, 1).wait()
    load(wo_hbm, wo_ref, 2).wait()
    for k in range(1, nx):
        token_copy(k).wait()
    for k in range(1, nx):
        wo_copy(k).start()

    total = jnp.zeros((rows, 1), jnp.float32)
    for j in range(nx):
        wide = xbuf[j].astype(jnp.float32)
        total = total + jnp.sum(wide * wide, axis=1, keepdims=True)
    inverse = lax.rsqrt(total / full + EPSILON)
    for j in range(nx):
        gain = gain_in_ref[:, j * width:(j + 1) * width].astype(jnp.float32)
        xbuf[j] = (xbuf[j].astype(jnp.float32) * inverse * gain).astype(jnp.bfloat16)

    def project(c):
        y = dot(xbuf[0], w_ref[c, :width, :])
        for j in range(1, nx):
            y = y + dot(xbuf[j], w_ref[c, j * width:(j + 1) * width, :])
        y = y.astype(jnp.bfloat16)
        (q_t, k_t, v_t)[c][...] = y.T.reshape(heads, DH, rows)
        if c == 2:
            for p in range(pairs):
                v_pair[p] = y[:, p * 2 * DH:(p + 1) * 2 * DH]

    low_lane = lax.broadcasted_iota(jnp.int32, (1, 2 * DH), 1) < DH
    tiles = feature_tiles()

    def expand(slot, u, edge, middle):
        wide = u.astype(jnp.float32)
        for j in range(rows // 128):
            lanes = slice(j * 128, (j + 1) * 128)
            for b in range(DH // TILE):
                tile = wide[b * TILE:(b + 1) * TILE, lanes]
                twice[slot, j, 2 * b * TILE:(2 * b + 1) * TILE, :] = tile
                twice[slot, j, (2 * b + 1) * TILE:(2 * b + 2) * TILE, :] = tile
        for j in range(rows // 128):
            lanes = slice(j * 128, (j + 1) * 128)
            rolled, held = None, None
            for at, (a, b, r) in enumerate(tiles):
                if held != (b, r):
                    low = 2 * b * TILE + r
                    rolled = twice[slot, j, low:low + TILE, :].astype(jnp.bfloat16)
                    held = (b, r)
                scaled = edge if a == b and r in (0, TILE // 2) else middle
                feat[slot, at * TILE:(at + 1) * TILE, lanes] = (
                    scaled[a * TILE:(a + 1) * TILE, lanes] * rolled
                )

    def make_state(p):
        both = jnp.concatenate([k_t[2 * p], k_t[2 * p + 1]], axis=0)
        values = v_pair[p]
        for a in range(2):
            u = k_t[2 * p + a]
            expand(a, u, u, u)
        step = FEATS // 4
        for i in range(4):
            at = slice(i * step, (i + 1) * step)
            state[p, at, :] = jnp.where(
                low_lane, dot(feat[0, at, :], values), dot(feat[1, at, :], values)
            )
        state[p, FEATS:, :] = jnp.where(
            low_lane, dot(k_t[2 * p], both, ((1,), (1,))), dot(k_t[2 * p + 1], both, ((1,), (1,)))
        )

    causal = lax.broadcasted_iota(jnp.int32, (rows, rows), 0) <= lax.broadcasted_iota(
        jnp.int32, (rows, rows), 1
    )

    def local(h, carry):
        scores = dot(k_t[h], q_t[h], ((0,), (0,)))
        weights = jnp.where(causal, scores * scores * (1.0 / DH), 0.0)
        den[h] = den[h] + jnp.sum(weights, axis=0, keepdims=True)
        num[h] = num[h] + dot(v_t[h], weights.astype(jnp.bfloat16))
        return carry

    def chain_copy(p, i):
        return pltpu.make_async_remote_copy(
            src_ref=outgoing.at[p, i], dst_ref=prefix.at[p, i],
            send_sem=chain_send.at[p, i], recv_sem=chain_recv.at[p, i],
            device_id=(right, hx), device_id_type=MESH,
        )

    def forward(p):
        for i in range(PARTS):
            copy = chain_copy(p, i)

            @pl.when(me > 0)
            def _():
                copy.wait_recv()

            @pl.when(me < n - 1)
            def _():
                own = state[p, i * piece:(i + 1) * piece, :]
                outgoing[p, i] = (prefix[p, i].astype(jnp.float32) + own).astype(jnp.bfloat16)
                copy.start()

    late = me >= n // 2
    early = jnp.logical_not(late)

    project(1)
    project(2)

    def first(p, carry):
        make_state(p)

        @pl.when(early)
        def _():
            forward(p)

        return carry

    lax.fori_loop(0, pairs, first, 0)
    project(0)
    lax.fori_loop(0, jnp.where(late, heads, 0), local, 0)

    def second(p, carry):
        @pl.when(late)
        def _():
            forward(p)

        whole = prefix[p].reshape(ROWS, 2 * DH).T
        for a in range(2):
            h = 2 * p + a
            u = q_t[h]
            expand(a, u, u * (1.0 / DH), u * (2.0 / DH))
            mine = whole[a * DH:(a + 1) * DH, :]
            num[h] = num[h] + dot(mine[:, :FEATS], feat[a])
            gram = dot(mine[:, FEATS:], u)
            den[h] = den[h] + jnp.sum(
                gram * u.astype(jnp.float32), axis=0, keepdims=True
            ) * (1.0 / DH)
        lax.fori_loop(2 * p, jnp.where(late, 2 * p, 2 * p + 2), local, 0)
        attended = jnp.concatenate(
            [num[2 * p + a] / (1.0 + den[2 * p + a]) for a in range(2)], axis=0
        )
        ss[0] = ss[0] + jnp.sum(attended * attended, axis=0, keepdims=True)
        gain = gain_mid_ref[:, pl.ds(pl.multiple_of(p * 2 * DH, 2 * DH), 2 * DH)]
        att[p] = (attended.T * gain.astype(jnp.float32)).astype(jnp.bfloat16)
        for k in range(1, nx):
            att_copy(k, p).start()
        return carry

    lax.fori_loop(0, pairs, second, 0)
    for k in range(1, nx):
        ss_copy(k).start()
    own = pl.ds(pl.multiple_of(hx * width, width), width)
    update = jnp.zeros((rows, width), jnp.float32)
    for p in range(pairs):
        update = update + dot(att[p], wo_ref[p * 2 * DH:(p + 1) * 2 * DH, own])
    for k in range(1, nx):
        wo_copy(k).wait()
        for p in range(pairs):
            att_copy(k, p).wait()
            update = update + dot(att_in[k, p], wo_in[k, p * 2 * DH:(p + 1) * 2 * DH, :])
    for k in range(1, nx):
        ss_copy(k).wait()
    squares = ss[0]
    for k in range(1, nx):
        squares = squares + ss[k]
    columns = jnp.broadcast_to(squares[:1], (128, rows)).T[:, :1]
    scale = lax.rsqrt(columns / full + EPSILON)
    out_ref[...] = (x_own[...].astype(jnp.float32) + update * scale).astype(jnp.bfloat16)

    @pl.when(me < n - 1)
    def _():
        for p in range(pairs):
            for i in range(PARTS):
                chain_copy(p, i).wait_send()


def shards(n, nx, tokens, w_qkv, w_out, gain_in, gain_mid):
    rows, width = tokens.shape
    features = w_qkv.shape[3]
    heads = features // DH
    pairs = heads // 2
    bf16, f32 = jnp.bfloat16, jnp.float32
    dma = pltpu.SemaphoreType.DMA
    return pl.pallas_call(
        functools.partial(kernel, n, nx),
        out_shape=jax.ShapeDtypeStruct((rows, width), bf16),
        in_specs=[pl.BlockSpec(memory_space=pl.ANY)] * 3
        + [pl.BlockSpec(memory_space=pltpu.VMEM)] * 2,
        out_specs=pl.BlockSpec(memory_space=pltpu.VMEM),
        scratch_shapes=[
            pltpu.VMEM((rows, width), bf16),
            pltpu.VMEM((3, nx * width, features), bf16),
            pltpu.VMEM((features, nx * width), bf16),
            pltpu.VMEM((nx, features, width), bf16),
            pltpu.VMEM((nx, rows, width), bf16),
            pltpu.VMEM((heads, DH, rows), bf16),
            pltpu.VMEM((heads, DH, rows), bf16),
            pltpu.VMEM((heads, DH, rows), bf16),
            pltpu.VMEM((pairs, rows, 2 * DH), bf16),
            pltpu.VMEM((2, FEATS, rows), bf16),
            pltpu.VMEM((2, rows // 128, 2 * DH, 128), f32),
            pltpu.VMEM((pairs, ROWS, 2 * DH), f32),
            pltpu.VMEM((pairs, PARTS, ROWS // PARTS, 2 * DH), bf16),
            pltpu.VMEM((pairs, PARTS, ROWS // PARTS, 2 * DH), bf16),
            pltpu.VMEM((heads, DH, rows), f32),
            pltpu.VMEM((heads, 1, rows), f32),
            pltpu.VMEM((pairs, rows, 2 * DH), bf16),
            pltpu.VMEM((nx, pairs, rows, 2 * DH), bf16),
            pltpu.VMEM((nx, 8, rows), f32),
            dma((3,)),
            dma((nx,)), dma((nx,)),
            dma((nx,)), dma((nx,)),
            dma((pairs, PARTS)), dma((pairs, PARTS)),
            dma((nx,)), dma((nx,)),
            dma((nx, pairs)), dma((nx, pairs)),
        ],
        compiler_params=pltpu.CompilerParams(
            collective_id=0, has_side_effects=True, vmem_limit_bytes=60 * 1024 * 1024
        ),
    )(tokens, w_qkv[0].transpose(1, 0, 2), w_out[0], gain_in, gain_mid)


def solution(mesh):
    placed = (
        P("seq", "head"),
        P(None, None, None, "head"),
        P(None, "head", None),
        P(),
        P(None, "head"),
    )
    return jax.shard_map(
        functools.partial(shards, mesh.shape["seq"], mesh.shape["head"]),
        mesh=mesh, in_specs=placed, out_specs=P("seq", "head"), check_vma=False,
    )
```

time: 104 us -> 82.8 us (0.80)
  Pallas kernels: 97.2 us -> 80 us
  local copies, waits for them, and re-layouts: 6.32 us -> 1.87 us
    pallas_call x1, Pallas kernels: 97.2 us -> 80 us  [shards(): pl.pallas_call(functools.partial(kernel, n, nx), out_shape=jax.ShapeDtype...]
    unnamed x11 -> x1, local copies, waits for them, and re-layouts: 6.32 us -> 1.87 us
where the time goes in v2:
time: 82.8 us; the launch traced here: 81.9 us
  Pallas kernels  80 us (97%)
  local copies, waits for them, and re-layouts  1.87 us (2%)
    pallas_call x1, Pallas kernels, shards(): pl.pallas_call(functools.partial(kernel, n, nx), out_shape=jax.ShapeDtype...  80 us
    unnamed x1, local copies, waits for them, and re-layouts  1.87 us

profile of v2, /device:TPU:29, one launch (start us, length us, event | category | flops | bytes accessed | tf_op | source)
XLA Modules:
  0.0 81.9 jit_solution(17103324745036957826)
XLA Ops:
  0.0 80.0 %shard_map.55 = bf16[512,512]{1,0:T(8,128)(2,1)} custom-call(bf16[512,512]{1,0:T(8,128)(2,1)} %x_ref.1, bf16[3,1024,512]{2,1,0:T(8,128)(2,1)} %bitcast.4, bf16[512,1024]{1,0:T(8,128)(2,1)} %bitcast.5, bf16[1,1024]{1,0:T(2,128)(2,1)} %gain_in_ref.1, bf16[1,512]{1,0:T(2,128)(2,1)} %gain_mid_ref.1), custom_call_target="tpu_custom_call" | custom-call | tf_op jit(solution)/shard_map/pallas_call | solution.py:279
  80.0 1.9 %copy.7 = bf16[512,512]{1,0:T(8,128)(2,1)} copy(bf16[512,512]{1,0:T(8,128)(2,1)} %shard_map.55) | data formatting | bytes 1048576

commit v3 on v2

--- a/solution.py
+++ b/solution.py
@@ -13,7 +13,8 @@
 TILE = 16
 FEATS = DH * (DH // 2 + 1)
 ROWS = FEATS + DH
-PARTS = 8
+GROUP = 4
+PIECE = ROWS // 8
 
 
 def dot(a, b, dims=((1,), (0,))):
@@ -32,9 +33,11 @@
 
 def kernel(
     n, nx, x_ref, w_hbm, wo_hbm, gain_in_ref, gain_mid_ref, out_ref,
-    x_own, w_ref, wo_ref, wo_in, xbuf, q_t, k_t, v_t, v_pair, feat, twice, state, prefix, outgoing,
+    x_own, w_ref, wo_ref, wo_in, xbuf, q_t, k_t, v_t, v_pair, feat, twice, state, prefix,
+    rs1_out, rs1_in, rs2_out, rs2_in, chain_out, chain_in, ag1_out, ag1_in, ag2_out,
     num, den, att, att_in, ss,
-    load_sem, x_send, x_recv, wo_send, wo_recv, chain_send, chain_recv, ss_send, ss_recv,
+    load_sem, x_send, x_recv, wo_send, wo_recv, rs1_send, rs1_recv, rs2_send, rs2_recv,
+    chain_send, chain_recv, ag1_send, ag1_recv, ag2_send, ag2_recv, ss_send, ss_recv,
     att_send, att_recv,
 ):
     me = lax.axis_index("seq")
@@ -44,8 +47,11 @@
     heads = features // DH
     pairs = heads // 2
     full = nx * width
-    piece = ROWS // PARTS
-    right, left = lax.rem(me + 1, n), lax.rem(me + n - 1, n)
+    parts = 8 * pairs // GROUP
+    planes = n // GROUP
+    z, y, c = lax.div(me, GROUP), lax.rem(lax.div(me, 2), 2), lax.rem(me, 2)
+    sibling, across_y = me + 1 - 2 * c, me + 2 - 4 * y
+    above, below = lax.rem(me + GROUP, n), lax.rem(me + n - GROUP, n)
 
     def load(src, dst, i):
         return pltpu.make_async_copy(src, dst, load_sem.at[i])
@@ -55,13 +61,13 @@
     load(wo_hbm, wo_ref, 2).start()
 
     barrier = pltpu.get_barrier_semaphore()
-    for neighbour in (left, right):
+    for neighbour in (sibling, across_y, above, below):
         pl.semaphore_signal(barrier, inc=1, device_id=(neighbour, hx), device_id_type=MESH)
     for k in range(1, nx):
         pl.semaphore_signal(
             barrier, inc=1, device_id=(me, lax.rem(hx + k, nx)), device_id_type=MESH
         )
-    pl.semaphore_wait(barrier, 2 + nx - 1)
+    pl.semaphore_wait(barrier, 4 + nx - 1)
 
     def across(src, dst, send, recv, k):
         return pltpu.make_async_remote_copy(
@@ -91,9 +97,9 @@
     den[...] = jnp.zeros_like(den)
     ss[0] = jnp.zeros_like(ss[0])
 
-    @pl.when(me == 0)
+    @pl.when(z == 0)
     def _():
-        prefix[...] = jnp.zeros_like(prefix)
+        chain_in[...] = jnp.zeros_like(chain_in)
 
     load(x_ref, x_own, 0).wait()
     xbuf[hx] = x_own[...]
@@ -113,15 +119,15 @@
         gain = gain_in_ref[:, j * width:(j + 1) * width].astype(jnp.float32)
         xbuf[j] = (xbuf[j].astype(jnp.float32) * inverse * gain).astype(jnp.bfloat16)
 
-    def project(c):
-        y = dot(xbuf[0], w_ref[c, :width, :])
+    def project(which):
+        got = dot(xbuf[0], w_ref[which, :width, :])
         for j in range(1, nx):
-            y = y + dot(xbuf[j], w_ref[c, j * width:(j + 1) * width, :])
-        y = y.astype(jnp.bfloat16)
-        (q_t, k_t, v_t)[c][...] = y.T.reshape(heads, DH, rows)
-        if c == 2:
+            got = got + dot(xbuf[j], w_ref[which, j * width:(j + 1) * width, :])
+        got = got.astype(jnp.bfloat16)
+        (q_t, k_t, v_t)[which][...] = got.T.reshape(heads, DH, rows)
+        if which == 2:
             for p in range(pairs):
-                v_pair[p] = y[:, p * 2 * DH:(p + 1) * 2 * DH]
+                v_pair[p] = got[:, p * 2 * DH:(p + 1) * 2 * DH]
 
     low_lane = lax.broadcasted_iota(jnp.int32, (1, 2 * DH), 1) < DH
     tiles = feature_tiles()
@@ -153,13 +159,13 @@
         for a in range(2):
             u = k_t[2 * p + a]
             expand(a, u, u, u)
-        step = FEATS // 4
-        for i in range(4):
-            at = slice(i * step, (i + 1) * step)
-            state[p, at, :] = jnp.where(
+        for i in range(8):
+            count = min(PIECE, FEATS - i * PIECE)
+            at = slice(i * PIECE, i * PIECE + count)
+            state[8 * p + i, :count, :] = jnp.where(
                 low_lane, dot(feat[0, at, :], values), dot(feat[1, at, :], values)
             )
-        state[p, FEATS:, :] = jnp.where(
+        state[8 * p + 7, PIECE - DH:, :] = jnp.where(
             low_lane, dot(k_t[2 * p], both, ((1,), (1,))), dot(k_t[2 * p + 1], both, ((1,), (1,)))
         )
 
@@ -174,52 +180,107 @@
         num[h] = num[h] + dot(v_t[h], weights.astype(jnp.bfloat16))
         return carry
 
-    def chain_copy(p, i):
+    def along(src, dst, send, recv, to):
         return pltpu.make_async_remote_copy(
-            src_ref=outgoing.at[p, i], dst_ref=prefix.at[p, i],
-            send_sem=chain_send.at[p, i], recv_sem=chain_recv.at[p, i],
-            device_id=(right, hx), device_id_type=MESH,
-        )
-
-    def forward(p):
-        for i in range(PARTS):
-            copy = chain_copy(p, i)
-
-            @pl.when(me > 0)
-            def _():
-                copy.wait_recv()
-
-            @pl.when(me < n - 1)
-            def _():
-                own = state[p, i * piece:(i + 1) * piece, :]
-                outgoing[p, i] = (prefix[p, i].astype(jnp.float32) + own).astype(jnp.bfloat16)
-                copy.start()
-
-    late = me >= n // 2
-    early = jnp.logical_not(late)
+            src_ref=src, dst_ref=dst, send_sem=send, recv_sem=recv,
+            device_id=(to, hx), device_id_type=MESH,
+        )
+
+    def rs1_copy(line, i):
+        return along(
+            rs1_out.at[line, i], rs1_in.at[line, i], rs1_send.at[line, i], rs1_recv.at[line, i],
+            sibling,
+        )
+
+    def rs2_copy(i):
+        return along(rs2_out.at[i], rs2_in.at[i], rs2_send.at[i], rs2_recv.at[i], across_y)
+
+    def chain_copy(i):
+        return along(chain_out.at[i], chain_in.at[i], chain_send.at[i], chain_recv.at[i], above)
+
+    def ag1_copy(i):
+        return along(ag1_out.at[i], ag1_in.at[i], ag1_send.at[i], ag1_recv.at[i], across_y)
+
+    def ag2_copy(line, i):
+        return along(
+            ag2_out.at[line, i], prefix.at[(2 * line + c) * parts + i], ag2_send.at[line, i],
+            ag2_recv.at[line, i], sibling,
+        )
+
+    def wide(value):
+        return value.astype(jnp.float32)
+
+    def narrow(value):
+        return value.astype(jnp.bfloat16)
+
+    is_second_core, is_second_line = c.astype(jnp.float32), y.astype(jnp.float32)
+
+    def make_unit(unit):
+        if pairs >= GROUP:
+            for j in range(pairs // GROUP):
+                make_state(unit * (pairs // GROUP) + j)
+
+    def give(line, unit):
+        make_unit(unit)
+        for i in range(parts):
+            rs1_out[line, i] = narrow(state[unit * parts + i])
+            rs1_copy(line, i).start()
+
+    def settle(line, i, chip_prefix):
+        at = (2 * line + c) * parts + i
+        prefix[at] = narrow(chip_prefix + is_second_core * wide(rs1_in[line, i]))
+        ag2_out[line, i] = narrow(chip_prefix + (1.0 - is_second_core) * state[at])
+        ag2_copy(line, i).start()
+
+    def own_part(i):
+        rs1_copy(y, i).wait_recv()
+        rs2_copy(i).wait_recv()
+
+        @pl.when(z > 0)
+        def _():
+            chain_copy(i).wait_recv()
+
+        mine = state[(2 * y + c) * parts + i] + wide(rs1_in[y, i])
+        other = wide(rs2_in[i])
+        before = wide(chain_in[i])
+
+        @pl.when(z < planes - 1)
+        def _():
+            chain_out[i] = narrow(before + mine + other)
+            chain_copy(i).start()
+
+        ag1_out[i] = narrow(before + (1.0 - is_second_line) * mine)
+        ag1_copy(i).start()
+        settle(y, i, before + is_second_line * other)
+
+    late = z >= planes // 2
 
     project(1)
     project(2)
-
-    def first(p, carry):
-        make_state(p)
-
-        @pl.when(early)
-        def _():
-            forward(p)
-
-        return carry
-
-    lax.fori_loop(0, pairs, first, 0)
+    if pairs < GROUP:
+        for p in range(pairs):
+            make_state(p)
+    far = 1 - y
+    give(far, 2 * far + 1 - c)
+    make_unit(2 * far + c)
+    for i in range(parts):
+        rs1_copy(far, i).wait_recv()
+        rs2_out[i] = narrow(state[(2 * far + c) * parts + i] + wide(rs1_in[far, i]))
+        rs2_copy(i).start()
+    give(y, 2 * y + 1 - c)
+    make_unit(2 * y + c)
     project(0)
     lax.fori_loop(0, jnp.where(late, heads, 0), local, 0)
-
-    def second(p, carry):
-        @pl.when(late)
-        def _():
-            forward(p)
-
-        whole = prefix[p].reshape(ROWS, 2 * DH).T
+    for i in range(parts):
+        own_part(i)
+
+    def far_parts():
+        for i in range(parts):
+            ag1_copy(i).wait_recv()
+            settle(far, i, wide(ag1_in[i]))
+
+    def query(p):
+        whole = prefix[pl.ds(8 * p, 8)].reshape(ROWS, 2 * DH).T
         for a in range(2):
             h = 2 * p + a
             u = q_t[h]
@@ -239,9 +300,34 @@
         att[p] = (attended.T * gain.astype(jnp.float32)).astype(jnp.bfloat16)
         for k in range(1, nx):
             att_copy(k, p).start()
-        return carry
-
-    lax.fori_loop(0, pairs, second, 0)
+
+    if pairs >= GROUP:
+
+        def turn(step, carry):
+            line = jnp.where(step < 2, y, far)
+            core = jnp.where(lax.rem(step, 2) == 0, c, 1 - c)
+
+            @pl.when(step == 1)
+            def _():
+                far_parts()
+
+            @pl.when(core != c)
+            def _():
+                for i in range(parts):
+                    ag2_copy(line, i).wait_recv()
+
+            for j in range(pairs // GROUP):
+                query((2 * line + core) * (pairs // GROUP) + j)
+            return carry
+
+        lax.fori_loop(0, GROUP, turn, 0)
+    else:
+        far_parts()
+        for i in range(parts):
+            for line in range(2):
+                ag2_copy(line, i).wait_recv()
+        for p in range(pairs):
+            query(p)
     for k in range(1, nx):
         ss_copy(k).start()
     own = pl.ds(pl.multiple_of(hx * width, width), width)
@@ -262,11 +348,17 @@
     scale = lax.rsqrt(columns / full + EPSILON)
     out_ref[...] = (x_own[...].astype(jnp.float32) + update * scale).astype(jnp.bfloat16)
 
-    @pl.when(me < n - 1)
+    for i in range(parts):
+        for line in range(2):
+            rs1_copy(line, i).wait_send()
+            ag2_copy(line, i).wait_send()
+        rs2_copy(i).wait_send()
+        ag1_copy(i).wait_send()
+
+    @pl.when(z < planes - 1)
     def _():
-        for p in range(pairs):
-            for i in range(PARTS):
-                chain_copy(p, i).wait_send()
+        for i in range(parts):
+            chain_copy(i).wait_send()
 
 
 def shards(n, nx, tokens, w_qkv, w_out, gain_in, gain_mid):
@@ -274,6 +366,7 @@
     features = w_qkv.shape[3]
     heads = features // DH
     pairs = heads // 2
+    parts = 8 * pairs // GROUP
     bf16, f32 = jnp.bfloat16, jnp.float32
     dma = pltpu.SemaphoreType.DMA
     return pl.pallas_call(
@@ -294,9 +387,17 @@
             pltpu.VMEM((pairs, rows, 2 * DH), bf16),
             pltpu.VMEM((2, FEATS, rows), bf16),
             pltpu.VMEM((2, rows // 128, 2 * DH, 128), f32),
-            pltpu.VMEM((pairs, ROWS, 2 * DH), f32),
-            pltpu.VMEM((pairs, PARTS, ROWS // PARTS, 2 * DH), bf16),
-            pltpu.VMEM((pairs, PARTS, ROWS // PARTS, 2 * DH), bf16),
+            pltpu.VMEM((8 * pairs, PIECE, 2 * DH), f32),
+            pltpu.VMEM((8 * pairs, PIECE, 2 * DH), bf16),
+            pltpu.VMEM((2, parts, PIECE, 2 * DH), bf16),
+            pltpu.VMEM((2, parts, PIECE, 2 * DH), bf16),
+            pltpu.VMEM((parts, PIECE, 2 * DH), bf16),
+            pltpu.VMEM((parts, PIECE, 2 * DH), bf16),
+            pltpu.VMEM((parts, PIECE, 2 * DH), bf16),
+            pltpu.VMEM((parts, PIECE, 2 * DH), bf16),
+            pltpu.VMEM((parts, PIECE, 2 * DH), bf16),
+            pltpu.VMEM((parts, PIECE, 2 * DH), bf16),
+            pltpu.VMEM((2, parts, PIECE, 2 * DH), bf16),
             pltpu.VMEM((heads, DH, rows), f32),
             pltpu.VMEM((heads, 1, rows), f32),
             pltpu.VMEM((pairs, rows, 2 * DH), bf16),
@@ -305,7 +406,11 @@
             dma((3,)),
             dma((nx,)), dma((nx,)),
             dma((nx,)), dma((nx,)),
-            dma((pairs, PARTS)), dma((pairs, PARTS)),
+            dma((2, parts)), dma((2, parts)),
+            dma((parts,)), dma((parts,)),
+            dma((parts,)), dma((parts,)),
+            dma((parts,)), dma((parts,)),
+            dma((2, parts)), dma((2, parts)),
             dma((nx,)), dma((nx,)),
             dma((nx, pairs)), dma((nx, pairs)),
         ],

time: 82.8 us -> 65.9 us (0.80)
  the two profiles are of different devices: /device:TPU:29 before, /device:TPU:0 now
where the time goes in v3:
time: 65.9 us; the launch traced here: 65.7 us
  Pallas kernels  63.8 us (97%)
  local copies, waits for them, and re-layouts  1.87 us (3%)
    pallas_call x1, Pallas kernels, shards(): pl.pallas_call(functools.partial(kernel, n, nx), out_shape=jax.ShapeDtype...  63.8 us
    unnamed x1, local copies, waits for them, and re-layouts  1.87 us

profile of v3, /device:TPU:0, one launch (start us, length us, event | category | flops | bytes accessed | tf_op | source)
XLA Modules:
  0.0 65.7 jit_solution(442605555644675856)
XLA Ops:
  0.0 63.8 %shard_map.55 = bf16[512,512]{1,0:T(8,128)(2,1)} custom-call(bf16[512,512]{1,0:T(8,128)(2,1)} %x_ref.1, bf16[3,1024,512]{2,1,0:T(8,128)(2,1)} %bitcast.4, bf16[512,1024]{1,0:T(8,128)(2,1)} %bitcast.5, bf16[1,1024]{1,0:T(2,128)(2,1)} %gain_in_ref.1, bf16[1,512]{1,0:T(2,128)(2,1)} %gain_mid_ref.1), custom_call_target="tpu_custom_call" | custom-call | tf_op jit(solution)/shard_map/pallas_call | solution.py:372
  63.8 1.9 %copy.7 = bf16[512,512]{1,0:T(8,128)(2,1)} copy(bf16[512,512]{1,0:T(8,128)(2,1)} %shard_map.55) | data formatting | bytes 1048576

commit v4 on v3

--- a/solution.py
+++ b/solution.py
@@ -14,6 +14,7 @@
 FEATS = DH * (DH // 2 + 1)
 ROWS = FEATS + DH
 GROUP = 4
+CHUNKS = 4
 PIECE = ROWS // 8
 
 
@@ -75,8 +76,11 @@
             device_id=(me, lax.rem(hx + k, nx)), device_id_type=MESH,
         )
 
-    def token_copy(k):
-        return across(x_ref, xbuf.at[hx], x_send.at[k], x_recv.at[k], k)
+    chunk = rows // CHUNKS
+
+    def token_copy(k, j):
+        at = pl.ds(j * chunk, chunk)
+        return across(x_ref.at[at], xbuf.at[hx, at], x_send.at[k, j], x_recv.at[k, j], k)
 
     def wo_copy(k):
         at = pl.multiple_of(lax.rem(hx + k, nx) * width, width)
@@ -90,8 +94,9 @@
     def att_copy(k, p):
         return across(att.at[p], att_in.at[k, p], att_send.at[k, p], att_recv.at[k, p], k)
 
-    for k in range(1, nx):
-        token_copy(k).start()
+    for j in range(CHUNKS):
+        for k in range(1, nx):
+            token_copy(k, j).start()
 
     num[...] = jnp.zeros_like(num)
     den[...] = jnp.zeros_like(den)
@@ -105,48 +110,49 @@
     xbuf[hx] = x_own[...]
     load(w_hbm, w_ref, 1).wait()
     load(wo_hbm, wo_ref, 2).wait()
-    for k in range(1, nx):
-        token_copy(k).wait()
+    for j in range(CHUNKS):
+        at = slice(j * chunk, (j + 1) * chunk)
+        for k in range(1, nx):
+            token_copy(k, j).wait()
+        blocks = [xbuf[i, at, :].astype(jnp.float32) for i in range(nx)]
+        total = sum(jnp.sum(block * block, axis=1, keepdims=True) for block in blocks)
+        inverse = lax.rsqrt(total / full + EPSILON)
+        normed = [
+            (block * inverse * gain_in_ref[:, i * width:(i + 1) * width].astype(jnp.float32)).astype(
+                jnp.bfloat16
+            )
+            for i, block in enumerate(blocks)
+        ]
+        for which in range(3):
+            got = dot(normed[0], w_ref[which, :width, :])
+            for i in range(1, nx):
+                got = got + dot(normed[i], w_ref[which, i * width:(i + 1) * width, :])
+            got = got.astype(jnp.bfloat16)
+            (q_t, k_t, v_t)[which][:, :, at] = got.T.reshape(heads, DH, chunk)
+            if which == 2:
+                for p in range(pairs):
+                    v_pair[p, at, :] = got[:, p * 2 * DH:(p + 1) * 2 * DH]
     for k in range(1, nx):
         wo_copy(k).start()
-
-    total = jnp.zeros((rows, 1), jnp.float32)
-    for j in range(nx):
-        wide = xbuf[j].astype(jnp.float32)
-        total = total + jnp.sum(wide * wide, axis=1, keepdims=True)
-    inverse = lax.rsqrt(total / full + EPSILON)
-    for j in range(nx):
-        gain = gain_in_ref[:, j * width:(j + 1) * width].astype(jnp.float32)
-        xbuf[j] = (xbuf[j].astype(jnp.float32) * inverse * gain).astype(jnp.bfloat16)
-
-    def project(which):
-        got = dot(xbuf[0], w_ref[which, :width, :])
-        for j in range(1, nx):
-            got = got + dot(xbuf[j], w_ref[which, j * width:(j + 1) * width, :])
-        got = got.astype(jnp.bfloat16)
-        (q_t, k_t, v_t)[which][...] = got.T.reshape(heads, DH, rows)
-        if which == 2:
-            for p in range(pairs):
-                v_pair[p] = got[:, p * 2 * DH:(p + 1) * 2 * DH]
 
     low_lane = lax.broadcasted_iota(jnp.int32, (1, 2 * DH), 1) < DH
     tiles = feature_tiles()
 
-    def expand(slot, u, edge, middle):
+    def expand(slot, spare, u, edge, middle):
         wide = u.astype(jnp.float32)
         for j in range(rows // 128):
             lanes = slice(j * 128, (j + 1) * 128)
             for b in range(DH // TILE):
                 tile = wide[b * TILE:(b + 1) * TILE, lanes]
-                twice[slot, j, 2 * b * TILE:(2 * b + 1) * TILE, :] = tile
-                twice[slot, j, (2 * b + 1) * TILE:(2 * b + 2) * TILE, :] = tile
+                twice[spare, j, 2 * b * TILE:(2 * b + 1) * TILE, :] = tile
+                twice[spare, j, (2 * b + 1) * TILE:(2 * b + 2) * TILE, :] = tile
         for j in range(rows // 128):
             lanes = slice(j * 128, (j + 1) * 128)
             rolled, held = None, None
             for at, (a, b, r) in enumerate(tiles):
                 if held != (b, r):
                     low = 2 * b * TILE + r
-                    rolled = twice[slot, j, low:low + TILE, :].astype(jnp.bfloat16)
+                    rolled = twice[spare, j, low:low + TILE, :].astype(jnp.bfloat16)
                     held = (b, r)
                 scaled = edge if a == b and r in (0, TILE // 2) else middle
                 feat[slot, at * TILE:(at + 1) * TILE, lanes] = (
@@ -158,7 +164,7 @@
         values = v_pair[p]
         for a in range(2):
             u = k_t[2 * p + a]
-            expand(a, u, u, u)
+            expand(a, a, u, u, u)
         for i in range(8):
             count = min(PIECE, FEATS - i * PIECE)
             at = slice(i * PIECE, i * PIECE + count)
@@ -169,15 +175,28 @@
             low_lane, dot(k_t[2 * p], both, ((1,), (1,))), dot(k_t[2 * p + 1], both, ((1,), (1,)))
         )
 
-    causal = lax.broadcasted_iota(jnp.int32, (rows, rows), 0) <= lax.broadcasted_iota(
-        jnp.int32, (rows, rows), 1
+    half = rows // 2
+    causal = lax.broadcasted_iota(jnp.int32, (half, half), 0) <= lax.broadcasted_iota(
+        jnp.int32, (half, half), 1
     )
 
     def local(h, carry):
-        scores = dot(k_t[h], q_t[h], ((0,), (0,)))
-        weights = jnp.where(causal, scores * scores * (1.0 / DH), 0.0)
-        den[h] = den[h] + jnp.sum(weights, axis=0, keepdims=True)
-        num[h] = num[h] + dot(v_t[h], weights.astype(jnp.bfloat16))
+        def weigh(s_at, t_at, masked):
+            scores = dot(k_t[h, :, s_at], q_t[h, :, t_at], ((0,), (0,)))
+            weights = scores * scores * (1.0 / DH)
+            if masked:
+                weights = jnp.where(causal, weights, 0.0)
+            total = jnp.sum(weights, axis=0, keepdims=True)
+            return total, dot(v_t[h, :, s_at], weights.astype(jnp.bfloat16))
+
+        low, high = slice(0, half), slice(half, rows)
+        den_a, num_a = weigh(low, low, True)
+        den_b, num_b = weigh(low, high, False)
+        den_c, num_c = weigh(high, high, True)
+        den[h, :, low] = den[h, :, low] + den_a
+        den[h, :, high] = den[h, :, high] + (den_b + den_c)
+        num[h, :, low] = num[h, :, low] + num_a
+        num[h, :, high] = num[h, :, high] + (num_b + num_c)
         return carry
 
     def along(src, dst, send, recv, to):
@@ -255,8 +274,6 @@
 
     late = z >= planes // 2
 
-    project(1)
-    project(2)
     if pairs < GROUP:
         for p in range(pairs):
             make_state(p)
@@ -269,29 +286,43 @@
         rs2_copy(i).start()
     give(y, 2 * y + 1 - c)
     make_unit(2 * y + c)
-    project(0)
+    per = pairs // GROUP
+
+    def fill(slot, spare, h):
+        u = q_t[h]
+        expand(slot, spare, u, u * (1.0 / DH), u * (2.0 / DH))
+
+    def fill_far(core, carry):
+        for j in range(per):
+            for a in range(2):
+                fill(2 + 2 * (per * core + j) + a, a, 2 * (per * (2 * far + core) + j) + a)
+        return carry
+
+    last = z == planes - 1
     lax.fori_loop(0, jnp.where(late, heads, 0), local, 0)
+    lax.fori_loop(0, jnp.where(last, 2, 0), fill_far, 0)
     for i in range(parts):
         own_part(i)
+    lax.fori_loop(0, jnp.where(late, 0, heads), local, 0)
 
     def far_parts():
         for i in range(parts):
             ag1_copy(i).wait_recv()
             settle(far, i, wide(ag1_in[i]))
 
-    def query(p):
+    def query(p, slot, filled):
         whole = prefix[pl.ds(8 * p, 8)].reshape(ROWS, 2 * DH).T
         for a in range(2):
             h = 2 * p + a
             u = q_t[h]
-            expand(a, u, u * (1.0 / DH), u * (2.0 / DH))
+            if not filled:
+                fill(slot + a, a, h)
             mine = whole[a * DH:(a + 1) * DH, :]
-            num[h] = num[h] + dot(mine[:, :FEATS], feat[a])
+            num[h] = num[h] + dot(mine[:, :FEATS], feat[slot + a])
             gram = dot(mine[:, FEATS:], u)
             den[h] = den[h] + jnp.sum(
                 gram * u.astype(jnp.float32), axis=0, keepdims=True
             ) * (1.0 / DH)
-        lax.fori_loop(2 * p, jnp.where(late, 2 * p, 2 * p + 2), local, 0)
         attended = jnp.concatenate(
             [num[2 * p + a] / (1.0 + den[2 * p + a]) for a in range(2)], axis=0
         )
@@ -303,31 +334,41 @@
 
     if pairs >= GROUP:
 
-        def turn(step, carry):
-            line = jnp.where(step < 2, y, far)
-            core = jnp.where(lax.rem(step, 2) == 0, c, 1 - c)
+        def near(step, carry):
+            core = jnp.where(step == 0, c, 1 - c)
 
             @pl.when(step == 1)
             def _():
-                far_parts()
-
-            @pl.when(core != c)
+                for i in range(parts):
+                    ag2_copy(y, i).wait_recv()
+
+            for j in range(per):
+                query((2 * y + core) * per + j, 0, False)
+            return carry
+
+        def distant(step, carry):
+            core = jnp.where(step == 0, c, 1 - c)
+
+            @pl.when(step == 1)
             def _():
                 for i in range(parts):
-                    ag2_copy(line, i).wait_recv()
-
-            for j in range(pairs // GROUP):
-                query((2 * line + core) * (pairs // GROUP) + j)
+                    ag2_copy(far, i).wait_recv()
+
+            for j in range(per):
+                query((2 * far + core) * per + j, 2 + 2 * (per * core + j), True)
             return carry
 
-        lax.fori_loop(0, GROUP, turn, 0)
+        lax.fori_loop(0, 2, near, 0)
+        lax.fori_loop(0, jnp.where(last, 0, 2), fill_far, 0)
+        far_parts()
+        lax.fori_loop(0, 2, distant, 0)
     else:
         far_parts()
         for i in range(parts):
             for line in range(2):
                 ag2_copy(line, i).wait_recv()
         for p in range(pairs):
-            query(p)
+            query(p, 0, False)
     for k in range(1, nx):
         ss_copy(k).start()
     own = pl.ds(pl.multiple_of(hx * width, width), width)
@@ -385,7 +426,7 @@
             pltpu.VMEM((heads, DH, rows), bf16),
             pltpu.VMEM((heads, DH, rows), bf16),
             pltpu.VMEM((pairs, rows, 2 * DH), bf16),
-            pltpu.VMEM((2, FEATS, rows), bf16),
+            pltpu.VMEM((2 + 4 * (pairs // GROUP), FEATS, rows), bf16),
             pltpu.VMEM((2, rows // 128, 2 * DH, 128), f32),
             pltpu.VMEM((8 * pairs, PIECE, 2 * DH), f32),
             pltpu.VMEM((8 * pairs, PIECE, 2 * DH), bf16),
@@ -404,7 +445,7 @@
             pltpu.VMEM((nx, pairs, rows, 2 * DH), bf16),
             pltpu.VMEM((nx, 8, rows), f32),
             dma((3,)),
-            dma((nx,)), dma((nx,)),
+            dma((nx, CHUNKS)), dma((nx, CHUNKS)),
             dma((nx,)), dma((nx,)),
             dma((2, parts)), dma((2, parts)),
             dma((parts,)), dma((parts,)),

time: 65.9 us -> 62.9 us (0.954)
  the two profiles are of different devices: /device:TPU:0 before, /device:TPU:29 now
where the time goes in v4:
time: 62.9 us; the launch traced here: 61.7 us
  Pallas kernels  59.8 us (95%)
  local copies, waits for them, and re-layouts  1.87 us (3%)
    pallas_call x1, Pallas kernels, shards(): pl.pallas_call(functools.partial(kernel, n, nx), out_shape=jax.ShapeDtype...  59.8 us
    unnamed x1, local copies, waits for them, and re-layouts  1.87 us

profile of v4, /device:TPU:29, one launch (start us, length us, event | category | flops | bytes accessed | tf_op | source)
XLA Modules:
  0.0 61.7 jit_solution(11838725626833015514)
XLA Ops:
  0.0 59.8 %shard_map.55 = bf16[512,512]{1,0:T(8,128)(2,1)} custom-call(bf16[512,512]{1,0:T(8,128)(2,1)} %x_ref.1, bf16[3,1024,512]{2,1,0:T(8,128)(2,1)} %bitcast.4, bf16[512,1024]{1,0:T(8,128)(2,1)} %bitcast.5, bf16[1,1024]{1,0:T(2,128)(2,1)} %gain_in_ref.1, bf16[1,512]{1,0:T(2,128)(2,1)} %gain_mid_ref.1), custom_call_target="tpu_custom_call" | custom-call | tf_op jit(solution)/shard_map/pallas_call | solution.py:413
  59.8 1.9 %copy.7 = bf16[512,512]{1,0:T(8,128)(2,1)} copy(bf16[512,512]{1,0:T(8,128)(2,1)} %shard_map.55) | data formatting | bytes 1048576

commit v5 on v4

--- a/solution.py
+++ b/solution.py
@@ -298,12 +298,12 @@
                 fill(2 + 2 * (per * core + j) + a, a, 2 * (per * (2 * far + core) + j) + a)
         return carry
 
-    last = z == planes - 1
-    lax.fori_loop(0, jnp.where(late, heads, 0), local, 0)
-    lax.fori_loop(0, jnp.where(last, 2, 0), fill_far, 0)
-    for i in range(parts):
+    def own_step(i, carry):
         own_part(i)
-    lax.fori_loop(0, jnp.where(late, 0, heads), local, 0)
+        return local(i, carry)
+
+    lax.fori_loop(0, jnp.where(late, 2, 0), fill_far, 0)
+    lax.fori_loop(0, parts, own_step, 0)
 
     def far_parts():
         for i in range(parts):
@@ -359,7 +359,7 @@
             return carry
 
         lax.fori_loop(0, 2, near, 0)
-        lax.fori_loop(0, jnp.where(last, 0, 2), fill_far, 0)
+        lax.fori_loop(0, jnp.where(late, 0, 2), fill_far, 0)
         far_parts()
         lax.fori_loop(0, 2, distant, 0)
     else:

time: 62.9 us -> 63.5 us (level)
  the two profiles are of different devices: /device:TPU:29 before, /device:TPU:26 now
where the time goes in v5:
time: 63.5 us; the launch traced here: 63.3 us
  Pallas kernels  61.4 us (97%)
  local copies, waits for them, and re-layouts  1.87 us (3%)
    pallas_call x1, Pallas kernels, shards(): pl.pallas_call(functools.partial(kernel, n, nx), out_shape=jax.ShapeDtype...  61.4 us
    unnamed x1, local copies, waits for them, and re-layouts  1.87 us

profile of v5, /device:TPU:26, one launch (start us, length us, event | category | flops | bytes accessed | tf_op | source)
XLA Modules:
  0.0 63.3 jit_solution(14847377770432930857)
XLA Ops:
  0.0 61.4 %shard_map.55 = bf16[512,512]{1,0:T(8,128)(2,1)} custom-call(bf16[512,512]{1,0:T(8,128)(2,1)} %x_ref.1, bf16[3,1024,512]{2,1,0:T(8,128)(2,1)} %bitcast.4, bf16[512,1024]{1,0:T(8,128)(2,1)} %bitcast.5, bf16[1,1024]{1,0:T(2,128)(2,1)} %gain_in_ref.1, bf16[1,512]{1,0:T(2,128)(2,1)} %gain_mid_ref.1), custom_call_target="tpu_custom_call" | custom-call | tf_op jit(solution)/shard_map/pallas_call | solution.py:413
  61.5 1.9 %copy.7 = bf16[512,512]{1,0:T(8,128)(2,1)} copy(bf16[512,512]{1,0:T(8,128)(2,1)} %shard_map.55) | data formatting | bytes 1048576
